TPU v7x, 32 devices: a whole 2x2x4 slice. The times are simulated.
32 devices in a mesh: groups: 2 (over x), tm: 16 (over z, y, core).
Axes of the slice: x: 2, y: 2, z: 4, core: 2. Of those that a mesh axis runs over, the one named last changes fastest.
Arguments:
- queries: bfloat16 [16384, 512], P(('groups', 'tm')), parts along dimension 0, may hold values from -6 to 6
- keys: bfloat16 [49152, 512], P(('groups', 'tm')), parts along dimension 0, may hold values from -6 to 6
- values: bfloat16 [49152, 512], P(('groups', 'tm')), parts along dimension 0, may hold values from -6 to 6
- out_grad: bfloat16 [16384, 512], P(('groups', 'tm')), parts along dimension 0, may hold values from -6 to 6
- band_start: int32 [32], P('groups'), parts along dimension 0, may hold values from 0 to 22528, as said below
- band_len: int32 [32], P('groups'), parts along dimension 0, may hold values from 1984 to 2048
Outputs:
- attended: bfloat16 [16384, 512], P(('groups', 'tm')), parts along dimension 0
- query_grad: bfloat16 [16384, 512], P(('groups', 'tm')), parts along dimension 0
- key_grad: bfloat16 [49152, 512], P(('groups', 'tm')), parts along dimension 0
- value_grad: bfloat16 [49152, 512], P(('groups', 'tm')), parts along dimension 0
There are 2 independent parts, one for each index of `groups`. A program takes and returns all parts, laid end to end along the dimension named above; each array names one. Nothing has to cross between parts.
Inputs may be any that keep to these rules, and one draw needn't show every extreme that they name: `band_start`: Nondecreasing; stretch c's band starts at c * 1536 - s with s from 128 to 3 * 512 // 4 (both taken in every draw), clipped to the range below.
All inputs are finite; a program needn't handle non-finite values.
Results may differ from a plain program's by a relative error of at most 0.012.
The roundings to bfloat16 on the way count: a program that leaves them out, or rounds other values in their place, can miss the bound.
Values may be sent and summed in bfloat16 or wider, within the bound.
A program may use at most 128 MiB of HBM per device.

v0:
```python
import jax
import jax.numpy as jnp
from jax import lax
from jax.sharding import PartitionSpec as P

DH = 64
UPC = 512
BAND = 2048
REACH = 512


SCORE_SCALE = 0.125
MASKED_SCORE = -1e30


def with_halo(array, sides, width):
    for axis, dim in sides:
        peers, length = (lax.axis_size(axis), array.shape[dim])
        up = [(i, (i + 1) % peers) for i in range(peers - 1)]
        down = [(j, i) for i, j in up]
        last = lax.slice_in_dim(array, length - width, length, axis=dim)
        first = lax.slice_in_dim(array, 0, width, axis=dim)
        before = lax.ppermute(last, axis, up)
        after = lax.ppermute(first, axis, down)
        array = jnp.concatenate([before, array, after], axis=dim)
    return array


def from_behind(block, axis, distance):
    devices = range(lax.axis_size(axis))
    route = [(i - distance, i) for i in devices if i - distance in devices]
    return lax.ppermute(block, axis, route)


def column_block(matrix, block_id):
    piece = lax.dynamic_slice_in_dim(matrix, block_id * (2 * DH), 2 * DH, 1)
    return piece.reshape(matrix.shape[0], 2, DH)


def merge_heads(stacked):
    return jnp.transpose(stacked, (1, 0, 2, 3)).reshape(stacked.shape[1], stacked.shape[0] * 2 * DH)


def block_scores(query_block, key_block, inside):
    scores = (
        jnp.einsum("uhd,bhd->hub", query_block, key_block, preferred_element_type=jnp.float32)
        * SCORE_SCALE
    )
    return jnp.where(inside[None, None, :], scores, MASKED_SCORE)


def grad_terms(weights, weights_low, query_block, grad_block, value_block, row_dot):
    weight_grad = jnp.einsum(
        "uhd,bhd->hub", grad_block, value_block, preferred_element_type=jnp.float32
    )
    score_grad = (weights * (weight_grad - row_dot[:, :, None]) * SCORE_SCALE).astype(jnp.bfloat16)
    key_term = jnp.einsum(
        "hub,uhd->bhd", score_grad, query_block, preferred_element_type=jnp.float32
    )
    value_term = jnp.einsum(
        "hub,uhd->bhd", weights_low, grad_block, preferred_element_type=jnp.float32
    )
    return (score_grad, key_term, value_term)


def owner_block(query_block, key_block, value_block, grad_block, inside):
    scores = block_scores(query_block, key_block, inside)
    row_max = jnp.max(scores, axis=-1, keepdims=True)
    log_total = row_max + jnp.log(jnp.sum(jnp.exp(scores - row_max), axis=-1, keepdims=True))
    weights = jnp.exp(scores - log_total)
    weights_low = weights.astype(jnp.bfloat16)
    attended = jnp.einsum(
        "hub,bhd->uhd", weights_low, value_block, preferred_element_type=jnp.float32
    ).astype(jnp.bfloat16)
    row_dot = jnp.einsum("uhd,uhd->hu", grad_block, attended, preferred_element_type=jnp.float32)
    score_grad, key_term, value_term = grad_terms(
        weights, weights_low, query_block, grad_block, value_block, row_dot
    )
    query_grad = jnp.einsum(
        "hub,bhd->uhd", score_grad, key_block, preferred_element_type=jnp.float32
    ).astype(jnp.bfloat16)
    return (attended, query_grad, key_term, value_term, log_total[:, :, 0], row_dot)


def on_device(queries, keys, values, out_grad, band_start, band_len):
    unit_rows, model_width = queries.shape
    frames = keys.shape[0]
    stretches = unit_rows // UPC
    blocks = model_width // (2 * DH)
    position = lax.axis_index("tm")
    first_frame = position * frames
    first_stretch = position * stretches
    wide_pair = with_halo(jnp.stack([keys, values]), (("tm", 1),), REACH)
    wide_span = frames + 2 * REACH
    key_total = jnp.zeros((wide_span, model_width), jnp.float32)
    value_total = jnp.zeros((wide_span, model_width), jnp.float32)
    attended_parts, query_parts, total_parts, dot_parts = ([], [], [], [])
    stretch_id = first_stretch + 0
    band_first = band_start[stretch_id]
    local_first = band_first - first_frame + REACH
    band_pair = lax.dynamic_slice_in_dim(wide_pair, local_first, BAND, 1)
    inside = jnp.arange(BAND, dtype=jnp.int32) < band_len[stretch_id]

    def per_block(block_id):
        return owner_block(
            column_block(queries, block_id),
            column_block(band_pair[0], block_id),
            column_block(band_pair[1], block_id),
            column_block(out_grad, block_id),
            inside,
        )

    attended, query_grad, key_term, value_term, log_total, row_dot = lax.map(
        per_block, jnp.arange(blocks, dtype=jnp.int32)
    )
    attended_parts.append(merge_heads(attended))
    query_parts.append(merge_heads(query_grad))
    total_parts.append(log_total.reshape(blocks * 2, UPC))
    dot_parts.append(row_dot.reshape(blocks * 2, UPC))
    key_total = lax.dynamic_update_slice_in_dim(key_total, merge_heads(key_term), local_first, 0)
    value_total = lax.dynamic_update_slice_in_dim(
        value_total, merge_heads(value_term), local_first, 0
    )
    attended_all = attended_parts[0]
    query_all = query_parts[0]
    key_own = key_total[REACH : REACH + frames]
    value_own = value_total[REACH : REACH + frames]
    lower_rims = jnp.stack([key_total[:REACH], value_total[:REACH]])
    upper_rims = jnp.stack([key_total[wide_span - REACH :], value_total[wide_span - REACH :]])
    from_above = from_behind(lower_rims, "tm", -1)
    from_below = from_behind(upper_rims.astype(jnp.bfloat16), "tm", 1).astype(upper_rims.dtype)
    key_own = key_own.at[:REACH].add(from_below[0]).at[frames - REACH :].add(from_above[0])
    value_own = value_own.at[:REACH].add(from_below[1]).at[frames - REACH :].add(from_above[1])
    return (attended_all, query_all, key_own.astype(jnp.bfloat16), value_own.astype(jnp.bfloat16))


def solution(mesh):
    return jax.shard_map(
        on_device,
        mesh=mesh,
        in_specs=(
            P(("groups", "tm"), None),
            P(("groups", "tm"), None),
            P(("groups", "tm"), None),
            P(("groups", "tm"), None),
            P("groups"),
            P("groups"),
        ),
        out_specs=(
            P(("groups", "tm"), None),
            P(("groups", "tm"), None),
            P(("groups", "tm"), None),
            P(("groups", "tm"), None),
        ),
        check_vma=False,
    )
```

profile of v0, /device:TPU:1, one launch (start us, length us, event | category | flops | bytes accessed | tf_op | source)
XLA Modules:
  0.0 242.4 jit_solution(10765662325490615874)
XLA Ops:
  5.6 4.5 %collective-permute-start = (bf16[2,512,512]{1,2,0:T(8,128)(2,1)}, bf16[2,512,512]{1,2,0:T(8,128)(2,1)}, u32[]{:S(2)}, u32[]{:S(2)}) collective-permute-start(bf16[2,512,512]{1,2,0:T(8,128)(2,1)} %get-tuple-element.193), channel_id=1, source_target_pairs={{0,1},{1,2},{2,3},{3,4},{4,5},{5,6},{6,7},{7,8},{8,9},{9,10},{10,1... | collective-permute-start | bytes 3145736 | tf_op jit(solution)/shard_map/ppermute | solution.py:23
  14.0 19.4 %collective-permute-done = bf16[2,512,512]{1,2,0:T(8,128)(2,1)} collective-permute-done((bf16[2,512,512]{1,2,0:T(8,128)(2,1)}, bf16[2,512,512]{1,2,0:T(8,128)(2,1)}, u32[]{:S(2)}, u32[]{:S(2)}) %collective-permute-start) | collective-permute-done | bytes 1048608 | tf_op jit(solution)/shard_map/ppermute | solution.py:23
  33.4 6.9 %fusion.16 = bf16[2,2048,512]{1,2,0:T(8,128)(2,1)} fusion(s32[]{:T(128)S(6)} %select_n.20, bf16[2,512,512]{1,2,0:T(8,128)(2,1)} %collective-permute-done, bf16[1,1536,512]{1,2,0:T(8,128)(2,1)S(1)} %bitcast.138, bf16[1,1536,512]{1,2,0:T(8,128)(2,1)S(1)} %bitcast.140, bf16[2,512,512]{1,2,0:T(8,128)(2,1)} %collective-permute-done.1), kind=kLoop, calls=%fused_computation.33 | loop fusion | flops 16777216 | bytes 9437188 | tf_op jit(solution)/shard_map/concatenate | solution.py:25
  40.4 101.8 %while.21 = (s32[]{:T(128)}, bf16[4,512,2,64]{1,3,2,0:T(8,128)(2,1)}, bf16[4,512,2,64]{1,3,2,0:T(8,128)(2,1)}, f32[4,2048,2,64]{1,3,2,0:T(8,128)}, f32[4,2048,2,...) while((s32[]{:T(128)}, ...), condition=%wide.region_3.4_spmd.clone, body=%wide.region_0.3_spmd.clone.sunk | while | flops 1657143296 | bytes 172156736 | solution.py:113
  41.6 2.7 %fusion.67 = (bf16[1,2048,512]{1,2,0:T(8,128)(2,1)S(1)}, bf16[1,2048,512]{1,2,0:T(8,128)(2,1)S(1)}) fusion(bf16[2,2048,512]{1,2,0:T(8,128)(2,1)} %get-tuple-element.314), kind=kLoop, calls=%fused_computation.57.clone.1 | loop fusion | bytes 8388608 | tf_op jit(solution)/shard_map/while/body/eval_jaxpr/slice | solution.py:107
  51.0 6.4 %fusion.72 = f32[4,2048,2,64]{1,3,2,0:T(8,128)} fusion(f32[4,2048,2,64]{1,3,2,0:T(8,128)} %get-tuple-element.299, s32[]{:T(128)} %get-tuple-element.295, bf16[512,2,64]{0,2,1:T(8,128)(2,1)S(1)} %bitcast.143, f32[2,512,2048]{2,1,0:T(8,128)} %copy-done, f32[2,512]{1,0:T(2,128)S(1)} %log_add_fusion.2, pred[2048]{0:T(1024)(128)(4,1)S(1)} %iota_compare_fusion.2), kind=kOutput, calls=%fused_computation.8.clone.1 | convolution fusion | flops 276824064 | bytes 9574912 | tf_op jit(solution)/shard_map/while/body/eval_jaxpr/hub,uhd->bhd/dot_general | solution.py:60
  57.4 2.5 %bitcast_dynamic-update-slice_fusion.2 = (bf16[4,512,2,64]{1,3,2,0:T(8,128)(2,1)}, bf16[2,64,512]{2,1,0:T(8,128)(2,1)S(1)}) fusion(bf16[4,512,2,64]{1,3,2,0:T(8,128)(2,1)} %get-tuple-element.296, s32[]{:T(128)} %get-tuple-element.295, bf16[2048,2,64]{0,2,1:T(8,128)(2,1)S(1)} %bitcast.141, f32[2,512,2048]{2,1,0:T(8,128)S(1)} %copy-done.1, ...), kind=kOutput, calls=%fused_computation.17.clone.1 | convolution fusion | flops 276889600 | bytes 9181696 | tf_op jit(solution)/shard_map/while/body/eval_jaxpr/hub,bhd->uhd/dot_general | solution.py:72
  59.9 3.0 %multiply_convert_fusion.2 = bf16[2,512,2048]{2,1,0:T(8,128)(2,1)S(1)} fusion(f32[2,512,2048]{2,1,0:T(8,128)S(1)} %copy-done.1, bf16[512,2,64]{0,2,1:T(8,128)(2,1)S(1)} %bitcast.144, bf16[2048,2,64]{0,2,1:T(8,128)(2,1)S(1)} %bitcast.142, f32[2,512]{1,0:T(2,128)S(1)} %fusion.69, f32[2,512]{1,0:T(2,128)S(1)} %log_add_fusion.2, ...), kind=kOutput, calls=%fused_computation.1.clone.1 | convolution fusion | flops 283115520 | bytes 13248512 | tf_op jit(solution)/shard_map/while/body/eval_jaxpr/uhd,bhd->hub/dot_general | solution.py:53
  67.1 2.7 %fusion.67 = (bf16[1,2048,512]{1,2,0:T(8,128)(2,1)S(1)}, bf16[1,2048,512]{1,2,0:T(8,128)(2,1)S(1)}) fusion(bf16[2,2048,512]{1,2,0:T(8,128)(2,1)} %get-tuple-element.314), kind=kLoop, calls=%fused_computation.57.clone.1 | loop fusion | bytes 8388608 | tf_op jit(solution)/shard_map/while/body/eval_jaxpr/slice | solution.py:107
  76.4 6.4 %fusion.72 = f32[4,2048,2,64]{1,3,2,0:T(8,128)} fusion(f32[4,2048,2,64]{1,3,2,0:T(8,128)} %get-tuple-element.299, s32[]{:T(128)} %get-tuple-element.295, bf16[512,2,64]{0,2,1:T(8,128)(2,1)S(1)} %bitcast.143, f32[2,512,2048]{2,1,0:T(8,128)} %copy-done, f32[2,512]{1,0:T(2,128)S(1)} %log_add_fusion.2, pred[2048]{0:T(1024)(128)(4,1)S(1)} %iota_compare_fusion.2), kind=kOutput, calls=%fused_computation.8.clone.1 | convolution fusion | flops 276824064 | bytes 9574912 | tf_op jit(solution)/shard_map/while/body/eval_jaxpr/hub,uhd->bhd/dot_general | solution.py:60
  82.8 2.5 %bitcast_dynamic-update-slice_fusion.2 = (bf16[4,512,2,64]{1,3,2,0:T(8,128)(2,1)}, bf16[2,64,512]{2,1,0:T(8,128)(2,1)S(1)}) fusion(bf16[4,512,2,64]{1,3,2,0:T(8,128)(2,1)} %get-tuple-element.296, s32[]{:T(128)} %get-tuple-element.295, bf16[2048,2,64]{0,2,1:T(8,128)(2,1)S(1)} %bitcast.141, f32[2,512,2048]{2,1,0:T(8,128)S(1)} %copy-done.1, ...), kind=kOutput, calls=%fused_computation.17.clone.1 | convolution fusion | flops 276889600 | bytes 9181696 | tf_op jit(solution)/shard_map/while/body/eval_jaxpr/hub,bhd->uhd/dot_general | solution.py:72
  85.4 2.9 %multiply_convert_fusion.2 = bf16[2,512,2048]{2,1,0:T(8,128)(2,1)S(1)} fusion(f32[2,512,2048]{2,1,0:T(8,128)S(1)} %copy-done.1, bf16[512,2,64]{0,2,1:T(8,128)(2,1)S(1)} %bitcast.144, bf16[2048,2,64]{0,2,1:T(8,128)(2,1)S(1)} %bitcast.142, f32[2,512]{1,0:T(2,128)S(1)} %fusion.69, f32[2,512]{1,0:T(2,128)S(1)} %log_add_fusion.2, ...), kind=kOutput, calls=%fused_computation.1.clone.1 | convolution fusion | flops 283115520 | bytes 13248512 | tf_op jit(solution)/shard_map/while/body/eval_jaxpr/uhd,bhd->hub/dot_general | solution.py:53
  92.5 2.7 %fusion.67 = (bf16[1,2048,512]{1,2,0:T(8,128)(2,1)S(1)}, bf16[1,2048,512]{1,2,0:T(8,128)(2,1)S(1)}) fusion(bf16[2,2048,512]{1,2,0:T(8,128)(2,1)} %get-tuple-element.314), kind=kLoop, calls=%fused_computation.57.clone.1 | loop fusion | bytes 8388608 | tf_op jit(solution)/shard_map/while/body/eval_jaxpr/slice | solution.py:107
  101.9 6.4 %fusion.72 = f32[4,2048,2,64]{1,3,2,0:T(8,128)} fusion(f32[4,2048,2,64]{1,3,2,0:T(8,128)} %get-tuple-element.299, s32[]{:T(128)} %get-tuple-element.295, bf16[512,2,64]{0,2,1:T(8,128)(2,1)S(1)} %bitcast.143, f32[2,512,2048]{2,1,0:T(8,128)} %copy-done, f32[2,512]{1,0:T(2,128)S(1)} %log_add_fusion.2, pred[2048]{0:T(1024)(128)(4,1)S(1)} %iota_compare_fusion.2), kind=kOutput, calls=%fused_computation.8.clone.1 | convolution fusion | flops 276824064 | bytes 9574912 | tf_op jit(solution)/shard_map/while/body/eval_jaxpr/hub,uhd->bhd/dot_general | solution.py:60
  108.2 2.5 %bitcast_dynamic-update-slice_fusion.2 = (bf16[4,512,2,64]{1,3,2,0:T(8,128)(2,1)}, bf16[2,64,512]{2,1,0:T(8,128)(2,1)S(1)}) fusion(bf16[4,512,2,64]{1,3,2,0:T(8,128)(2,1)} %get-tuple-element.296, s32[]{:T(128)} %get-tuple-element.295, bf16[2048,2,64]{0,2,1:T(8,128)(2,1)S(1)} %bitcast.141, f32[2,512,2048]{2,1,0:T(8,128)S(1)} %copy-done.1, ...), kind=kOutput, calls=%fused_computation.17.clone.1 | convolution fusion | flops 276889600 | bytes 9181696 | tf_op jit(solution)/shard_map/while/body/eval_jaxpr/hub,bhd->uhd/dot_general | solution.py:72
  110.8 3.0 %multiply_convert_fusion.2 = bf16[2,512,2048]{2,1,0:T(8,128)(2,1)S(1)} fusion(f32[2,512,2048]{2,1,0:T(8,128)S(1)} %copy-done.1, bf16[512,2,64]{0,2,1:T(8,128)(2,1)S(1)} %bitcast.144, bf16[2048,2,64]{0,2,1:T(8,128)(2,1)S(1)} %bitcast.142, f32[2,512]{1,0:T(2,128)S(1)} %fusion.69, f32[2,512]{1,0:T(2,128)S(1)} %log_add_fusion.2, ...), kind=kOutput, calls=%fused_computation.1.clone.1 | convolution fusion | flops 283115520 | bytes 13248512 | tf_op jit(solution)/shard_map/while/body/eval_jaxpr/uhd,bhd->hub/dot_general | solution.py:53
  118.0 2.7 %fusion.67 = (bf16[1,2048,512]{1,2,0:T(8,128)(2,1)S(1)}, bf16[1,2048,512]{1,2,0:T(8,128)(2,1)S(1)}) fusion(bf16[2,2048,512]{1,2,0:T(8,128)(2,1)} %get-tuple-element.314), kind=kLoop, calls=%fused_computation.57.clone.1 | loop fusion | bytes 8388608 | tf_op jit(solution)/shard_map/while/body/eval_jaxpr/slice | solution.py:107
  127.3 6.4 %fusion.72 = f32[4,2048,2,64]{1,3,2,0:T(8,128)} fusion(f32[4,2048,2,64]{1,3,2,0:T(8,128)} %get-tuple-element.299, s32[]{:T(128)} %get-tuple-element.295, bf16[512,2,64]{0,2,1:T(8,128)(2,1)S(1)} %bitcast.143, f32[2,512,2048]{2,1,0:T(8,128)} %copy-done, f32[2,512]{1,0:T(2,128)S(1)} %log_add_fusion.2, pred[2048]{0:T(1024)(128)(4,1)S(1)} %iota_compare_fusion.2), kind=kOutput, calls=%fused_computation.8.clone.1 | convolution fusion | flops 276824064 | bytes 9574912 | tf_op jit(solution)/shard_map/while/body/eval_jaxpr/hub,uhd->bhd/dot_general | solution.py:60
  133.7 2.5 %bitcast_dynamic-update-slice_fusion.2 = (bf16[4,512,2,64]{1,3,2,0:T(8,128)(2,1)}, bf16[2,64,512]{2,1,0:T(8,128)(2,1)S(1)}) fusion(bf16[4,512,2,64]{1,3,2,0:T(8,128)(2,1)} %get-tuple-element.296, s32[]{:T(128)} %get-tuple-element.295, bf16[2048,2,64]{0,2,1:T(8,128)(2,1)S(1)} %bitcast.141, f32[2,512,2048]{2,1,0:T(8,128)S(1)} %copy-done.1, ...), kind=kOutput, calls=%fused_computation.17.clone.1 | convolution fusion | flops 276889600 | bytes 9181696 | tf_op jit(solution)/shard_map/while/body/eval_jaxpr/hub,bhd->uhd/dot_general | solution.py:72
  136.3 3.0 %multiply_convert_fusion.2 = bf16[2,512,2048]{2,1,0:T(8,128)(2,1)S(1)} fusion(f32[2,512,2048]{2,1,0:T(8,128)S(1)} %copy-done.1, bf16[512,2,64]{0,2,1:T(8,128)(2,1)S(1)} %bitcast.144, bf16[2048,2,64]{0,2,1:T(8,128)(2,1)S(1)} %bitcast.142, f32[2,512]{1,0:T(2,128)S(1)} %fusion.69, f32[2,512]{1,0:T(2,128)S(1)} %log_add_fusion.2, ...), kind=kOutput, calls=%fused_computation.1.clone.1 | convolution fusion | flops 283115520 | bytes 13248512 | tf_op jit(solution)/shard_map/while/body/eval_jaxpr/uhd,bhd->hub/dot_general | solution.py:53
  142.2 5.4 %copy.22 = f32[2048,512]{1,0:T(8,128)} copy(f32[2048,512]{0,1:T(8,128)} %bitcast.145) | data formatting | bytes 8388608 | tf_op jit(solution)/shard_map/reshape | solution.py:41
  147.6 5.3 %copy.23 = f32[2048,512]{1,0:T(8,128)} copy(f32[2048,512]{0,1:T(8,128)} %bitcast.146) | data formatting | bytes 8388608 | tf_op jit(solution)/shard_map/reshape | solution.py:41
  153.0 3.0 %broadcast.65.clone = f32[2560,512]{1,0:T(8,128)} broadcast(f32[]{:T(128)} %constant.135.clone.1), dimensions={} | broadcast | bytes 5242884 | tf_op jit(solution)/shard_map/broadcast.7
  156.0 11.9 %dynamic_update_slice.20 = f32[2560,512]{1,0:T(8,128)} dynamic-update-slice(f32[2560,512]{1,0:T(8,128)} %broadcast.65.clone, f32[2048,512]{1,0:T(8,128)} %copy.22, s32[]{:T(128)S(6)} %select_n.20, s32[]{:T(128)} %constant.133.clone.1) | dynamic-update-slice | bytes 8388612 | tf_op jit(solution)/shard_map/dynamic_update_slice | solution.py:120
  167.9 3.0 %broadcast.65.clone.1 = f32[2560,512]{1,0:T(8,128)} broadcast(f32[]{:T(128)} %constant.135.clone.1), dimensions={} | broadcast | bytes 5242884 | tf_op jit(solution)/shard_map/broadcast.7
  170.9 12.0 %dynamic_update_slice.21 = f32[2560,512]{1,0:T(8,128)} dynamic-update-slice(f32[2560,512]{1,0:T(8,128)} %broadcast.65.clone.1, f32[2048,512]{1,0:T(8,128)} %copy.23, s32[]{:T(128)S(6)} %select_n.20, s32[]{:T(128)} %constant.133.clone.1) | dynamic-update-slice | bytes 8388612 | tf_op jit(solution)/shard_map/dynamic_update_slice | solution.py:121
  184.7 4.7 %collective-permute-start.2 = (bf16[2,512,512]{2,1,0:T(8,128)(2,1)S(1)}, bf16[2,512,512]{2,1,0:T(8,128)(2,1)S(1)}, u32[]{:S(2)}, u32[]{:S(2)}) collective-permute-start(bf16[2,512,512]{2,1,0:T(8,128)(2,1)S(1)} %pad_maximum_fusion.3), channel_id=1, source_target_pairs={{0,1},{1,2},{2,3},{3,4},{4,5},{5,6},{6,7},{7,8},{8,9},{9,10},{10,1... | collective-permute-start | bytes 3145736 | tf_op jit(solution)/shard_map/ppermute | solution.py:32
  189.3 2.2 slice.140
  191.9 9.2 %collective-permute-done.2 = bf16[2,512,512]{2,1,0:T(8,128)(2,1)S(1)} collective-permute-done((bf16[2,512,512]{2,1,0:T(8,128)(2,1)S(1)}, bf16[2,512,512]{2,1,0:T(8,128)(2,1)S(1)}, u32[]{:S(2)}, u32[]{:S(2)}) %collective-permute-start.2) | collective-permute-done | bytes 1048608 | tf_op jit(solution)/shard_map/ppermute | solution.py:32
  201.3 2.3 slice_bitcast_fusion.4
  212.8 22.4 %collective-permute-done.3 = f32[2,512,512]{2,1,0:T(8,128)} collective-permute-done((f32[2,512,512]{2,1,0:T(8,128)}, f32[2,512,512]{2,1,0:T(8,128)}, u32[]{:S(2)}, u32[]{:S(2)}) %collective-permute-start.3) | collective-permute-done | bytes 2097184 | tf_op jit(solution)/shard_map/ppermute | solution.py:32
  235.2 3.4 %fusion.19 = (f32[1536,512]{1,0:T(8,128)}, f32[1536,512]{1,0:T(8,128)S(1)}) fusion(f32[1536,512]{1,0:T(8,128)} %copy-done.3, f32[2,512,512]{2,1,0:T(8,128)} %collective-permute-done.3, f32[1536,512]{1,0:T(8,128)S(1)} %get-tuple-element.191), kind=kLoop, calls=%fused_computation.38 | loop fusion | flops 524288 | bytes 6291456 | tf_op jit(solution)/shard_map/scatter-add | solution.py:133
  (112 shorter events, 63.9 us)
Async XLA Ops:
  2.4 9.8 %copy-start.7 = (s32[16]{0:T(128)S(1)}, s32[16]{0:T(128)}, u32[]{:S(2)}) copy-start(s32[16]{0:T(128)} %param.20) | copy-start | bytes 196
  2.4 11.0 %copy-start.8 = (s32[16]{0:T(128)S(1)}, s32[16]{0:T(128)}, u32[]{:S(2)}) copy-start(s32[16]{0:T(128)} %param.21) | copy-start | bytes 196
  5.6 27.8 %collective-permute-start = (bf16[2,512,512]{1,2,0:T(8,128)(2,1)}, bf16[2,512,512]{1,2,0:T(8,128)(2,1)}, u32[]{:S(2)}, u32[]{:S(2)}) collective-permute-start(bf16[2,512,512]{1,2,0:T(8,128)(2,1)} %get-tuple-element.193), channel_id=1, source_target_pairs={{0,1},{1,2},{2,3},{3,4},{4,5},{5,6},{6,7},{7,8},{8,9},{9,10},{10,1... | collective-permute-start | bytes 3145736 | tf_op jit(solution)/shard_map/ppermute | solution.py:23
  10.2 23.3 %collective-permute-start.1 = (bf16[2,512,512]{1,2,0:T(8,128)(2,1)}, bf16[2,512,512]{1,2,0:T(8,128)(2,1)}, u32[]{:S(2)}, u32[]{:S(2)}) collective-permute-start(bf16[2,512,512]{1,2,0:T(8,128)(2,1)} %get-tuple-element.192), channel_id=1, source_target_pairs={{1,0},{2,1},{3,2},{4,3},{5,4},{6,5},{7,6},{8,7},{9,8},{10,9},{11,1... | collective-permute-start | bytes 3145736 | tf_op jit(solution)/shard_map/ppermute | solution.py:24
  47.6 3.2 %copy-start = (f32[2,512,2048]{2,1,0:T(8,128)}, f32[2,512,2048]{2,1,0:T(8,128)S(1)}, u32[]{:S(2)}) copy-start(f32[2,512,2048]{2,1,0:T(8,128)S(1)} %get-tuple-element.276) | copy-start | bytes 25165828 | tf_op jit(solution)/shard_map/while
  51.0 6.4 %copy-start.1 = (f32[2,512,2048]{2,1,0:T(8,128)S(1)}, f32[2,512,2048]{2,1,0:T(8,128)}, u32[]{:S(2)}) copy-start(f32[2,512,2048]{2,1,0:T(8,128)} %copy-done) | copy-start | bytes 25165828 | tf_op jit(solution)/shard_map/while
  59.9 3.0 %copy-start.5 = (f32[4,2048,2,64]{1,3,2,0:T(8,128)S(1)}, f32[4,2048,2,64]{1,3,2,0:T(8,128)}, u32[]{:S(2)}) copy-start(f32[4,2048,2,64]{1,3,2,0:T(8,128)} %get-tuple-element.298) | copy-start | bytes 12582916 | tf_op jit(solution)/shard_map/while
  63.8 2.1 copy-start.6
  73.1 3.2 %copy-start = (f32[2,512,2048]{2,1,0:T(8,128)}, f32[2,512,2048]{2,1,0:T(8,128)S(1)}, u32[]{:S(2)}) copy-start(f32[2,512,2048]{2,1,0:T(8,128)S(1)} %get-tuple-element.276) | copy-start | bytes 25165828 | tf_op jit(solution)/shard_map/while
  76.4 6.4 %copy-start.1 = (f32[2,512,2048]{2,1,0:T(8,128)S(1)}, f32[2,512,2048]{2,1,0:T(8,128)}, u32[]{:S(2)}) copy-start(f32[2,512,2048]{2,1,0:T(8,128)} %copy-done) | copy-start | bytes 25165828 | tf_op jit(solution)/shard_map/while
  85.4 3.0 %copy-start.5 = (f32[4,2048,2,64]{1,3,2,0:T(8,128)S(1)}, f32[4,2048,2,64]{1,3,2,0:T(8,128)}, u32[]{:S(2)}) copy-start(f32[4,2048,2,64]{1,3,2,0:T(8,128)} %get-tuple-element.298) | copy-start | bytes 12582916 | tf_op jit(solution)/shard_map/while
  89.2 2.1 copy-start.6
  98.5 3.2 %copy-start = (f32[2,512,2048]{2,1,0:T(8,128)}, f32[2,512,2048]{2,1,0:T(8,128)S(1)}, u32[]{:S(2)}) copy-start(f32[2,512,2048]{2,1,0:T(8,128)S(1)} %get-tuple-element.276) | copy-start | bytes 25165828 | tf_op jit(solution)/shard_map/while
  101.9 6.4 %copy-start.1 = (f32[2,512,2048]{2,1,0:T(8,128)S(1)}, f32[2,512,2048]{2,1,0:T(8,128)}, u32[]{:S(2)}) copy-start(f32[2,512,2048]{2,1,0:T(8,128)} %copy-done) | copy-start | bytes 25165828 | tf_op jit(solution)/shard_map/while
  110.8 3.0 %copy-start.5 = (f32[4,2048,2,64]{1,3,2,0:T(8,128)S(1)}, f32[4,2048,2,64]{1,3,2,0:T(8,128)}, u32[]{:S(2)}) copy-start(f32[4,2048,2,64]{1,3,2,0:T(8,128)} %get-tuple-element.298) | copy-start | bytes 12582916 | tf_op jit(solution)/shard_map/while
  114.7 2.1 copy-start.6
  124.0 3.2 %copy-start = (f32[2,512,2048]{2,1,0:T(8,128)}, f32[2,512,2048]{2,1,0:T(8,128)S(1)}, u32[]{:S(2)}) copy-start(f32[2,512,2048]{2,1,0:T(8,128)S(1)} %get-tuple-element.276) | copy-start | bytes 25165828 | tf_op jit(solution)/shard_map/while
  127.3 6.4 %copy-start.1 = (f32[2,512,2048]{2,1,0:T(8,128)S(1)}, f32[2,512,2048]{2,1,0:T(8,128)}, u32[]{:S(2)}) copy-start(f32[2,512,2048]{2,1,0:T(8,128)} %copy-done) | copy-start | bytes 25165828 | tf_op jit(solution)/shard_map/while
  136.3 3.0 %copy-start.5 = (f32[4,2048,2,64]{1,3,2,0:T(8,128)S(1)}, f32[4,2048,2,64]{1,3,2,0:T(8,128)}, u32[]{:S(2)}) copy-start(f32[4,2048,2,64]{1,3,2,0:T(8,128)} %get-tuple-element.298) | copy-start | bytes 12582916 | tf_op jit(solution)/shard_map/while
  140.1 2.1 copy-start.6
  184.5 7.0 %copy-start.2 = (f32[2560,512]{1,0:T(8,128)S(1)}, f32[2560,512]{1,0:T(8,128)}, u32[]{:S(2)}) copy-start(f32[2560,512]{1,0:T(8,128)} %dynamic_update_slice.21) | copy-start | bytes 15728644
  184.7 16.4 %collective-permute-start.2 = (bf16[2,512,512]{2,1,0:T(8,128)(2,1)S(1)}, bf16[2,512,512]{2,1,0:T(8,128)(2,1)S(1)}, u32[]{:S(2)}, u32[]{:S(2)}) collective-permute-start(bf16[2,512,512]{2,1,0:T(8,128)(2,1)S(1)} %pad_maximum_fusion.3), channel_id=1, source_target_pairs={{0,1},{1,2},{2,3},{3,4},{4,5},{5,6},{6,7},{7,8},{8,9},{9,10},{10,1... | collective-permute-start | bytes 3145736 | tf_op jit(solution)/shard_map/ppermute | solution.py:32
  203.6 1.6 copy-start.3
  206.8 28.4 %collective-permute-start.3 = (f32[2,512,512]{2,1,0:T(8,128)}, f32[2,512,512]{2,1,0:T(8,128)}, u32[]{:S(2)}, u32[]{:S(2)}) collective-permute-start(f32[2,512,512]{2,1,0:T(8,128)} %pad_maximum_fusion), channel_id=1, source_target_pairs={{1,0},{2,1},{3,2},{4,3},{5,4},{6,5},{7,6},{8,7},{9,8},{10,9},{11,1... | collective-permute-start | bytes 6291464 | tf_op jit(solution)/shard_map/ppermute | solution.py:32
  238.6 2.5 %copy-start.4 = (f32[1536,512]{1,0:T(8,128)S(1)}, f32[1536,512]{1,0:T(8,128)}, u32[]{:S(2)}) copy-start(f32[1536,512]{1,0:T(8,128)} %get-tuple-element.196) | copy-start | bytes 9437188
where the time goes:
time: 244 us; the launch traced here: 242 us
  local copies, waits for them, and re-layouts  80.2 us (33%)
  matrix products  64.7 us (27%)
  waiting for transfers between devices  51 us (21%)
  other arithmetic  29 us (12%)
  starting transfers between devices  13 us (5%)
  loops' own time  3.02 us (1%)
    ppermute x2, waiting for transfers between devices, from_behind(): return lax.ppermute(block, axis, route)  31.6 us
    dot_general x4, matrix products, grad_terms(): jnp.einsum('hub,uhd->bhd', weights_low, grad_block, preferred_element_typ...  25.5 us
    ppermute x1, waiting for transfers between devices, with_halo(): before = lax.ppermute(last, axis, up)  19.4 us
    dynamic_update_slice x1, local copies, waits for them, and re-layouts, on_device(): lax.dynamic_update_slice_in_dim(value_total, merge_heads(value_term), loc...  12 us
    dynamic_update_slice x1, local copies, waits for them, and re-layouts, on_device(): lax.dynamic_update_slice_in_dim(key_total, merge_heads(key_term), local_f...  11.9 us
    dot_general x4, matrix products, grad_terms(): jnp.einsum('uhd,bhd->hub', grad_block, value_block, preferred_element_typ...  11.8 us
    slice x4, local copies, waits for them, and re-layouts, per_block(): band_pair[0]  10.9 us
    reshape x2, local copies, waits for them, and re-layouts, merge_heads(): jnp.transpose(stacked, (1, 0, 2, 3))  10.8 us
  transfers between devices with their start and end apart: 4, of which 3 were waited for; matrix products, arithmetic and copies ran while one was open for 3% of the time, Pallas kernels for 0%

commit v1 on v0

v1 whole, which is shorter than its diff:
```python
import functools
import math

import jax
import jax.numpy as jnp
from jax import lax
from jax.experimental import pallas as pl
from jax.experimental.pallas import tpu as pltpu
from jax.sharding import PartitionSpec as P

DH = 64
PAIR = 2 * DH
BAND = 2048
REACH = 512
NEAR = 384
FAR = REACH - NEAR
CHUNK = 256
EXPONENT = 0.125 * math.log2(math.e)
MASKED = -1e30
BF16 = jnp.bfloat16
F32 = jnp.float32


def dot(a, b):
    return jnp.dot(a, b, preferred_element_type=F32)


def kernel(
    n, start_ref, len_ref, q_ref, g_ref, k_hbm, v_hbm,
    att_ref, qg_ref, kg_ref, vg_ref,
    wide, bias, probs, maxima, qtx, qm, gt8, gm, att_t, qg_t, totals,
    out_rim, in_rim,
    local_sem, halo_send, halo_recv, far_send, far_recv,
    rim_send, rim_recv, rfar_send, rfar_recv,
):
    me = lax.axis_index("tm")
    units, width = q_ref.shape
    frames = k_hbm.shape[0]
    pairs = width // PAIR
    span = frames + 2 * REACH
    has_lo = me > 0
    has_hi = me < n - 1
    first = me == 0
    last = me == n - 1
    top = REACH + frames

    def remote(src, dst, send, recv, target):
        return pltpu.make_async_remote_copy(
            src_ref=src, dst_ref=dst, send_sem=send, recv_sem=recv,
            device_id={"tm": target}, device_id_type=pl.DeviceIdType.MESH,
        )

    def halo(t, g, way):
        if way == 0:
            src, dst, target = top - NEAR, REACH - NEAR, me + 1
        else:
            src, dst, target = REACH, top, me - 1
        return remote(
            wide.at[t, g, pl.ds(src, NEAR)], wide.at[t, g, pl.ds(dst, NEAR)],
            halo_send.at[t, g, way], halo_recv.at[t, g, way], target,
        )

    def halo_far(t, g, way):
        if way == 0:
            src, dst, target = top - REACH, 0, me + 1
        else:
            src, dst, target = REACH + NEAR, top + NEAR, me - 1
        return remote(
            wide.at[t, g, pl.ds(src, FAR)], wide.at[t, g, pl.ds(dst, FAR)],
            far_send.at[t, g, way], far_recv.at[t, g, way], target,
        )

    def rim(t, g, way):
        off, target = (0, me + 1) if way == 0 else (FAR, me - 1)
        return remote(
            out_rim.at[t, g, way, pl.ds(off, NEAR)], in_rim.at[t, g, way, pl.ds(off, NEAR)],
            rim_send.at[t, g, way], rim_recv.at[t, g, way], target,
        )

    def rim_far(t, g, way):
        off, target = (NEAR, me + 1) if way == 0 else (0, me - 1)
        return remote(
            out_rim.at[t, g, way, pl.ds(off, FAR)], in_rim.at[t, g, way, pl.ds(off, FAR)],
            rfar_send.at[t, g, way], rfar_recv.at[t, g, way], target,
        )

    def local(t, g):
        src = (k_hbm, v_hbm)[t]
        return pltpu.make_async_copy(
            src.at[:, pl.ds(g * PAIR, PAIR)], wide.at[t, g, pl.ds(REACH, frames)],
            local_sem.at[t, g],
        )

    for g in range(pairs):
        for t in range(2):
            local(t, g).start()

    barrier = pltpu.get_barrier_semaphore()

    @pl.when(has_lo)
    def _():
        pl.semaphore_signal(
            barrier, inc=1, device_id={"tm": me - 1}, device_id_type=pl.DeviceIdType.MESH)

    @pl.when(has_hi)
    def _():
        pl.semaphore_signal(
            barrier, inc=1, device_id={"tm": me + 1}, device_id_type=pl.DeviceIdType.MESH)

    pl.semaphore_wait(barrier, has_lo.astype(jnp.int32) + has_hi.astype(jnp.int32))

    @pl.when(first)
    def _():
        in_rim[:, :, 0] = jnp.zeros((2, pairs, REACH, PAIR), BF16)

    @pl.when((me > 1))
    def _():
        in_rim[:, :, 0, NEAR:] = jnp.zeros((2, pairs, FAR, PAIR), BF16)

    @pl.when(last)
    def _():
        in_rim[:, :, 1] = jnp.zeros((2, pairs, REACH, PAIR), BF16)

    @pl.when((me < n - 2))
    def _():
        in_rim[:, :, 1, :FAR] = jnp.zeros((2, pairs, FAR, PAIR), BF16)

    for g in range(pairs):
        for t in range(2):
            local(t, g).wait()

            @pl.when(has_hi)
            def _():
                halo(t, g, 0).start()

            @pl.when(me == n - 2)
            def _():
                halo_far(t, g, 0).start()

            @pl.when(has_lo)
            def _():
                halo(t, g, 1).start()

            @pl.when(me == 1)
            def _():
                halo_far(t, g, 1).start()

    band_first = start_ref[me] - me * frames + REACH
    band_end = band_first + len_ref[me]
    row_id = lax.broadcasted_iota(jnp.int32, (span, PAIR), 0)
    inside = (row_id >= band_first) & (row_id < band_end)
    bias[...] = jnp.where(inside, 0.0, MASKED).astype(BF16)

    row0 = jnp.where(first, REACH, jnp.where(last, 0, FAR))
    chunks = jnp.where(first | last, BAND, frames + 2 * NEAR) // CHUNK

    def rows_of(i):
        return pl.ds(pl.multiple_of(row0 + i * CHUNK, 128), CHUNK)

    def finish(g):
        for t, out in ((0, kg_ref), (1, vg_ref)):
            @pl.when(has_lo)
            def _():
                rim(t, g, 0).wait_recv()

            @pl.when(me == 1)
            def _():
                rim_far(t, g, 0).wait_recv()

            @pl.when(has_hi)
            def _():
                rim(t, g, 1).wait_recv()

            @pl.when(me == n - 2)
            def _():
                rim_far(t, g, 1).wait_recv()

            cols = pl.ds(pl.multiple_of(g * PAIR, PAIR), PAIR)
            own = totals[t, g, REACH:2 * REACH]
            out[:REACH, cols] = (own + in_rim[t, g, 0].astype(F32)).astype(BF16)
            mid = totals[t, g, 2 * REACH:top - REACH]
            out[REACH:frames - REACH, cols] = mid.astype(BF16)
            own = totals[t, g, top - REACH:top]
            out[frames - REACH:, cols] = (own + in_rim[t, g, 1].astype(F32)).astype(BF16)

    def per_pair(g, _):
        cols = pl.ds(pl.multiple_of(g * PAIR, PAIR), PAIR)
        q = q_ref[:, cols].astype(F32)
        grad = g_ref[:, cols].astype(F32)
        q_t = q.T
        grad_t = grad.T
        feature = lax.broadcasted_iota(jnp.int32, (PAIR, units), 0)
        lane = lax.broadcasted_iota(jnp.int32, (units, PAIR), 1)
        for e in range(2):
            mine_t = (feature < DH) == (e == 0)
            mine = (lane < DH) == (e == 0)
            qtx[e, :PAIR] = jnp.where(mine_t, q_t, 0.0).astype(BF16)
            qtx[e, PAIR:] = jnp.where(feature == 0, 1.0, 0.0).astype(BF16)
            qm[e] = jnp.where(mine, q, 0.0).astype(BF16)
            gt8[e] = jnp.where(mine_t, grad_t * 0.125, 0.0).astype(BF16)
            gm[e] = jnp.where(mine, grad, 0.0).astype(BF16)

        for t in range(2):
            @pl.when(has_lo)
            def _():
                halo(t, g, 0).wait_recv()

            @pl.when(last)
            def _():
                halo_far(t, g, 0).wait_recv()

            @pl.when(has_hi)
            def _():
                halo(t, g, 1).wait_recv()

            @pl.when(first)
            def _():
                halo_far(t, g, 1).wait_recv()

        def scores(i, carry):
            rows = rows_of(i)
            key = jnp.concatenate([wide[0, g, rows], bias[rows]], axis=1)
            new = []
            for e in range(2):
                peak, total = carry[e]
                s = dot(key, qtx[e])
                peak_now = jnp.maximum(peak, jnp.max(s, axis=0, keepdims=True))
                prob = jnp.exp2((s - peak_now) * EXPONENT)
                probs[e, rows] = prob
                maxima[e, i] = peak_now
                total = total * jnp.exp2((peak - peak_now) * EXPONENT)
                new.append((peak_now, total + jnp.sum(prob, axis=0, keepdims=True)))
            return tuple(new)

        none = (jnp.full((1, units), -1e38, F32), jnp.zeros((1, units), F32))
        stats = lax.fori_loop(0, chunks, scores, (none, none))
        inverse = [1.0 / stats[e][1] for e in range(2)]

        def factor(e, i):
            return jnp.exp2((maxima[e, i] - stats[e][0]) * EXPONENT) * inverse[e]

        att_t[...] = jnp.zeros_like(att_t)
        qg_t[...] = jnp.zeros_like(qg_t)

        def attend(i, _):
            rows = rows_of(i)
            value_t = wide[1, g, rows].T
            term = None
            for e in range(2):
                low = (probs[e, rows] * factor(e, i)).astype(BF16)
                half = slice(e * DH, (e + 1) * DH)
                att_t[half] += dot(value_t[half], low)
                part = dot(low, gm[e])
                term = part if term is None else term + part
            totals[1, g, rows] = term
            return 0

        lax.fori_loop(0, chunks, attend, 0)

        attended = att_t[...].astype(BF16).astype(F32)
        att_ref[:, cols] = attended.T.astype(BF16)
        product = attended * grad_t * 0.125
        row_dot = [
            jnp.sum(product[e * DH:(e + 1) * DH], axis=0, keepdims=True) for e in range(2)
        ]

        def backward(i, _):
            rows = rows_of(i)
            value = wide[1, g, rows]
            key_t = wide[0, g, rows].T
            term = None
            for e in range(2):
                weight = probs[e, rows] * factor(e, i)
                score_grad = (weight * (dot(value, gt8[e]) - row_dot[e])).astype(BF16)
                half = slice(e * DH, (e + 1) * DH)
                qg_t[half] += dot(key_t[half], score_grad)
                part = dot(score_grad, qm[e])
                term = part if term is None else term + part
            totals[0, g, rows] = term
            return 0

        lax.fori_loop(0, chunks, backward, 0)
        qg_ref[:, cols] = qg_t[...].T.astype(BF16)

        for t in range(2):
            @pl.when(has_hi)
            def _():
                out_rim[t, g, 0, :NEAR] = totals[t, g, top:top + NEAR].astype(BF16)
                rim(t, g, 0).start()

            @pl.when(first)
            def _():
                out_rim[t, g, 0, NEAR:] = totals[t, g, top + NEAR:].astype(BF16)
                rim_far(t, g, 0).start()

            @pl.when(has_lo)
            def _():
                out_rim[t, g, 1, FAR:] = totals[t, g, FAR:REACH].astype(BF16)
                rim(t, g, 1).start()

            @pl.when(last)
            def _():
                out_rim[t, g, 1, :FAR] = totals[t, g, :FAR].astype(BF16)
                rim_far(t, g, 1).start()

        @pl.when(g > 0)
        def _():
            finish(g - 1)

        return 0

    lax.fori_loop(0, pairs, per_pair, 0)
    finish(pairs - 1)

    for g in range(pairs):
        for t in range(2):
            @pl.when(has_hi)
            def _():
                halo(t, g, 0).wait_send()
                rim(t, g, 0).wait_send()

            @pl.when(has_lo)
            def _():
                halo(t, g, 1).wait_send()
                rim(t, g, 1).wait_send()

            @pl.when(me == n - 2)
            def _():
                halo_far(t, g, 0).wait_send()

            @pl.when(me == 1)
            def _():
                halo_far(t, g, 1).wait_send()

            @pl.when(first)
            def _():
                rim_far(t, g, 0).wait_send()

            @pl.when(last)
            def _():
                rim_far(t, g, 1).wait_send()


def on_device(n, queries, keys, values, out_grad, band_start, band_len):
    units, width = queries.shape
    frames = keys.shape[0]
    pairs = width // PAIR
    span = frames + 2 * REACH
    dma = pltpu.SemaphoreType.DMA
    vmem = pl.BlockSpec(memory_space=pltpu.VMEM)
    smem = pl.BlockSpec(memory_space=pltpu.SMEM)
    anywhere = pl.BlockSpec(memory_space=pl.ANY)
    return pl.pallas_call(
        functools.partial(kernel, n),
        out_shape=(
            jax.ShapeDtypeStruct((units, width), BF16),
            jax.ShapeDtypeStruct((units, width), BF16),
            jax.ShapeDtypeStruct((frames, width), BF16),
            jax.ShapeDtypeStruct((frames, width), BF16),
        ),
        in_specs=[smem, smem, vmem, vmem, anywhere, anywhere],
        out_specs=(vmem, vmem, vmem, vmem),
        scratch_shapes=[
            pltpu.VMEM((2, pairs, span, PAIR), BF16),
            pltpu.VMEM((span, PAIR), BF16),
            pltpu.VMEM((2, span, units), F32),
            pltpu.VMEM((2, span // CHUNK, 1, units), F32),
            pltpu.VMEM((2, 2 * PAIR, units), BF16),
            pltpu.VMEM((2, units, PAIR), BF16),
            pltpu.VMEM((2, PAIR, units), BF16),
            pltpu.VMEM((2, units, PAIR), BF16),
            pltpu.VMEM((PAIR, units), F32),
            pltpu.VMEM((PAIR, units), F32),
            pltpu.VMEM((2, pairs, span, PAIR), F32),
            pltpu.VMEM((2, pairs, 2, REACH, PAIR), BF16),
            pltpu.VMEM((2, pairs, 2, REACH, PAIR), BF16),
            dma((2, pairs)),
        ] + [dma((2, pairs, 2))] * 8,
        compiler_params=pltpu.CompilerParams(
            collective_id=0, has_side_effects=True, vmem_limit_bytes=56 * 2**20
        ),
        name="banded",
    )(band_start, band_len, queries, out_grad, keys, values)


def solution(mesh):
    rows = P(("groups", "tm"), None)
    return jax.shard_map(
        functools.partial(on_device, mesh.shape["tm"]),
        mesh=mesh,
        in_specs=(rows, rows, rows, rows, P("groups"), P("groups")),
        out_specs=(rows, rows, rows, rows),
        check_vma=False,
    )
```

time: 244 us -> 91.4 us (0.37)
  Pallas kernels: 0 us -> 83.5 us
  local copies, waits for them, and re-layouts: 80.2 us -> 6.98 us
  matrix products: 64.7 us -> 0 us
  waiting for transfers between devices: 51 us -> 0 us
  other arithmetic: 29 us -> 0 us
  starting transfers between devices: 13 us -> 0 us
  loops' own time: 3.02 us -> 0 us
    pallas_call x0 -> x1, Pallas kernels: none -> 83.5 us  [on_device(): pl.pallas_call(functools.partial(kernel, n), out_shape=(jax.ShapeDtypeStr...]
    dot_general x24 -> x0, matrix products: 64.7 us -> none  [the longest x4 25.5 us: grad_terms(): jnp.einsum('hub,uhd->bhd', weights_low, grad_block, preferred_element_typ...]
    ppermute x4 -> x0, waiting for transfers between devices: 51 us -> none  [the longest x2 31.6 us: from_behind(): return lax.ppermute(block, axis, route)]
    dynamic_update_slice x2 -> x0, local copies, waits for them, and re-layouts: 23.9 us -> none  [the longest x1 12 us: on_device(): lax.dynamic_update_slice_in_dim(value_total, merge_heads(value_term), loc...]
    slice x6 -> x0, local copies, waits for them, and re-layouts: 13.4 us -> none  [the longest x4 10.9 us: per_block(): band_pair[0]]
    ppermute x4 -> x0, starting transfers between devices: 13 us -> none  [the longest x2 6.57 us: from_behind(): return lax.ppermute(block, axis, route)]
    reshape x2 -> x0, local copies, waits for them, and re-layouts: 10.8 us -> none  [merge_heads(): jnp.transpose(stacked, (1, 0, 2, 3))]
    dynamic_slice x22 -> x0, local copies, waits for them, and re-layouts: 8.77 us -> none  [the longest x16 5.22 us: column_block(): piece = lax.dynamic_slice_in_dim(matrix, block_id * (2 * DH), 2 * DH, 1)]
  transfers between devices with their start and end apart: 4 -> 0, of which waited for: 3 -> 0; matrix products, arithmetic and copies ran while one was open for 3% -> 0% of each run, Pallas kernels for 0% -> 0%
where the time goes in v1:
time: 91.4 us; the launch traced here: 91.2 us
  Pallas kernels  83.5 us (91%)
  local copies, waits for them, and re-layouts  6.98 us (8%)
    pallas_call x1, Pallas kernels, on_device(): pl.pallas_call(functools.partial(kernel, n), out_shape=(jax.ShapeDtypeStr...  83.5 us
    unnamed x8, local copies, waits for them, and re-layouts  6.98 us

profile of v1, /device:TPU:1, one launch (start us, length us, event | category | flops | bytes accessed | tf_op | source)
XLA Modules:
  0.0 91.2 jit_solution(4496619810755329556)
XLA Ops:
  0.6 83.5 %banded.1 = (bf16[512,512]{1,0:T(8,128)(2,1)}, bf16[512,512]{1,0:T(8,128)(2,1)}, bf16[1536,512]{1,0:T(8,128)(2,1)}, bf16[1536,512]{1,0:T(8,128)(2,1)}) custom-call(s32[16]{0:T(128)} %start_ref.1, s32[16]{0:T(128)} %len_ref.1, bf16[512,512]{1,0:T(8,128)(2,1)} %q_ref.1, bf16[512,512]{1,0:T(8,128)(2,1)} %g_ref.1, bf16[1536,512]{1,0:T(8,128)(2,1)} %k_hbm.1, ...), custom_call_target="tpu_custom_call" | custom-call | tf_op jit(solution)/shard_map/banded/pallas_call | solution.py:353
  84.2 0.0 copy-start.1
  84.2 2.0 %copy.14 = bf16[512,512]{1,0:T(8,128)(2,1)} copy(bf16[512,512]{1,0:T(8,128)(2,1)} %get-tuple-element.8) | data formatting | bytes 1048576
  86.2 1.9 %copy.15 = bf16[512,512]{1,0:T(8,128)(2,1)} copy(bf16[512,512]{1,0:T(8,128)(2,1)} %get-tuple-element.9) | data formatting | bytes 1048576
  88.0 0.0 copy-done.1
  88.0 0.0 copy-start
  88.0 1.1 %copy.16 = bf16[1536,512]{1,0:T(8,128)(2,1)} copy(bf16[1536,512]{1,0:T(8,128)(2,1)S(1)} %copy-done.1) | data formatting | bytes 3145728
  89.2 0.8 copy-done
  90.0 1.1 %copy.17 = bf16[1536,512]{1,0:T(8,128)(2,1)} copy(bf16[1536,512]{1,0:T(8,128)(2,1)S(1)} %copy-done) | data formatting | bytes 3145728
Async XLA Ops:
  84.2 3.9 %copy-start.1 = (bf16[1536,512]{1,0:T(8,128)(2,1)S(1)}, bf16[1536,512]{1,0:T(8,128)(2,1)}, u32[]{:S(2)}) copy-start(bf16[1536,512]{1,0:T(8,128)(2,1)} %get-tuple-element.10) | copy-start | bytes 4718596
  88.0 2.0 %copy-start = (bf16[1536,512]{1,0:T(8,128)(2,1)S(1)}, bf16[1536,512]{1,0:T(8,128)(2,1)}, u32[]{:S(2)}) copy-start(bf16[1536,512]{1,0:T(8,128)(2,1)} %get-tuple-element.11) | copy-start | bytes 4718596

commit v2 on v1

--- a/solution.py
+++ b/solution.py
@@ -14,7 +14,8 @@
 REACH = 512
 NEAR = 384
 FAR = REACH - NEAR
-CHUNK = 256
+CHUNK = 1152
+UNROLL = 1
 EXPONENT = 0.125 * math.log2(math.e)
 MASKED = -1e30
 BF16 = jnp.bfloat16
@@ -111,6 +112,14 @@
 
     @pl.when(first)
     def _():
+        wide[:, :, 2 * FAR:REACH] = jnp.zeros((2, pairs, REACH - 2 * FAR, PAIR), BF16)
+
+    @pl.when(last)
+    def _():
+        wide[:, :, top:top + 2 * FAR] = jnp.zeros((2, pairs, 2 * FAR, PAIR), BF16)
+
+    @pl.when(first)
+    def _():
         in_rim[:, :, 0] = jnp.zeros((2, pairs, REACH, PAIR), BF16)
 
     @pl.when((me > 1))
@@ -151,8 +160,8 @@
     inside = (row_id >= band_first) & (row_id < band_end)
     bias[...] = jnp.where(inside, 0.0, MASKED).astype(BF16)
 
-    row0 = jnp.where(first, REACH, jnp.where(last, 0, FAR))
-    chunks = jnp.where(first | last, BAND, frames + 2 * NEAR) // CHUNK
+    row0 = jnp.where(first, 2 * FAR, jnp.where(last, 0, FAR))
+    chunks = (frames + 2 * NEAR) // CHUNK
 
     def rows_of(i):
         return pl.ds(pl.multiple_of(row0 + i * CHUNK, 128), CHUNK)
@@ -233,7 +242,7 @@
             return tuple(new)
 
         none = (jnp.full((1, units), -1e38, F32), jnp.zeros((1, units), F32))
-        stats = lax.fori_loop(0, chunks, scores, (none, none))
+        stats = lax.fori_loop(0, chunks, scores, (none, none), unroll=UNROLL)
         inverse = [1.0 / stats[e][1] for e in range(2)]
 
         def factor(e, i):
@@ -255,7 +264,7 @@
             totals[1, g, rows] = term
             return 0
 
-        lax.fori_loop(0, chunks, attend, 0)
+        lax.fori_loop(0, chunks, attend, 0, unroll=UNROLL)
 
         attended = att_t[...].astype(BF16).astype(F32)
         att_ref[:, cols] = attended.T.astype(BF16)
@@ -279,7 +288,7 @@
             totals[0, g, rows] = term
             return 0
 
-        lax.fori_loop(0, chunks, backward, 0)
+        lax.fori_loop(0, chunks, backward, 0, unroll=UNROLL)
         qg_ref[:, cols] = qg_t[...].T.astype(BF16)
 
         for t in range(2):
@@ -364,7 +373,7 @@
             pltpu.VMEM((2, pairs, span, PAIR), BF16),
             pltpu.VMEM((span, PAIR), BF16),
             pltpu.VMEM((2, span, units), F32),
-            pltpu.VMEM((2, span // CHUNK, 1, units), F32),
+            pltpu.VMEM((2, span // CHUNK + 1, 1, units), F32),
             pltpu.VMEM((2, 2 * PAIR, units), BF16),
             pltpu.VMEM((2, units, PAIR), BF16),
             pltpu.VMEM((2, PAIR, units), BF16),

time: 91.4 us -> 70.7 us (0.77)
  Pallas kernels: 83.5 us -> 62.8 us
    pallas_call x1, Pallas kernels: 83.5 us -> 62.8 us  [on_device(): pl.pallas_call(functools.partial(kernel, n), out_shape=(jax.ShapeDtypeStr...]
where the time goes in v2:
time: 70.7 us; the launch traced here: 70.4 us
  Pallas kernels  62.8 us (89%)
  local copies, waits for them, and re-layouts  6.98 us (10%)
    pallas_call x1, Pallas kernels, on_device(): pl.pallas_call(functools.partial(kernel, n), out_shape=(jax.ShapeDtypeStr...  62.8 us
    unnamed x8, local copies, waits for them, and re-layouts  6.98 us

profile of v2, /device:TPU:1, one launch (start us, length us, event | category | flops | bytes accessed | tf_op | source)
XLA Modules:
  0.0 70.4 jit_solution(10865596499521884209)
XLA Ops:
  0.6 62.8 %banded.1 = (bf16[512,512]{1,0:T(8,128)(2,1)}, bf16[512,512]{1,0:T(8,128)(2,1)}, bf16[1536,512]{1,0:T(8,128)(2,1)}, bf16[1536,512]{1,0:T(8,128)(2,1)}) custom-call(s32[16]{0:T(128)} %start_ref.1, s32[16]{0:T(128)} %len_ref.1, bf16[512,512]{1,0:T(8,128)(2,1)} %q_ref.1, bf16[512,512]{1,0:T(8,128)(2,1)} %g_ref.1, bf16[1536,512]{1,0:T(8,128)(2,1)} %k_hbm.1, ...), custom_call_target="tpu_custom_call" | custom-call | tf_op jit(solution)/shard_map/banded/pallas_call | solution.py:362
  63.4 0.0 copy-start.1
  63.5 2.0 %copy.14 = bf16[512,512]{1,0:T(8,128)(2,1)} copy(bf16[512,512]{1,0:T(8,128)(2,1)} %get-tuple-element.8) | data formatting | bytes 1048576
  65.4 1.9 %copy.15 = bf16[512,512]{1,0:T(8,128)(2,1)} copy(bf16[512,512]{1,0:T(8,128)(2,1)} %get-tuple-element.9) | data formatting | bytes 1048576
  67.3 0.0 copy-done.1
  67.3 0.0 copy-start
  67.3 1.1 %copy.16 = bf16[1536,512]{1,0:T(8,128)(2,1)} copy(bf16[1536,512]{1,0:T(8,128)(2,1)S(1)} %copy-done.1) | data formatting | bytes 3145728
  68.5 0.8 %copy-done = bf16[1536,512]{1,0:T(8,128)(2,1)S(1)} copy-done((bf16[1536,512]{1,0:T(8,128)(2,1)S(1)}, bf16[1536,512]{1,0:T(8,128)(2,1)}, u32[]{:S(2)}) %copy-start) | copy-done | bytes 1572888
  69.3 1.1 %copy.17 = bf16[1536,512]{1,0:T(8,128)(2,1)} copy(bf16[1536,512]{1,0:T(8,128)(2,1)S(1)} %copy-done) | data formatting | bytes 3145728
Async XLA Ops:
  63.4 3.9 %copy-start.1 = (bf16[1536,512]{1,0:T(8,128)(2,1)S(1)}, bf16[1536,512]{1,0:T(8,128)(2,1)}, u32[]{:S(2)}) copy-start(bf16[1536,512]{1,0:T(8,128)(2,1)} %get-tuple-element.10) | copy-start | bytes 4718596
  67.3 2.0 %copy-start = (bf16[1536,512]{1,0:T(8,128)(2,1)S(1)}, bf16[1536,512]{1,0:T(8,128)(2,1)}, u32[]{:S(2)}) copy-start(bf16[1536,512]{1,0:T(8,128)(2,1)} %get-tuple-element.11) | copy-start | bytes 4718596

commit v3 on v2

--- a/solution.py
+++ b/solution.py
@@ -16,6 +16,7 @@
 FAR = REACH - NEAR
 CHUNK = 1152
 UNROLL = 1
+PARTS = 4
 EXPONENT = 0.125 * math.log2(math.e)
 MASKED = -1e30
 BF16 = jnp.bfloat16
@@ -167,7 +168,12 @@
         return pl.ds(pl.multiple_of(row0 + i * CHUNK, 128), CHUNK)
 
     def finish(g):
-        for t, out in ((0, kg_ref), (1, vg_ref)):
+        cols = pl.ds(pl.multiple_of(g * PAIR, PAIR), PAIR)
+        for t, out in ((1, vg_ref), (0, kg_ref)):
+            mid = totals[t, g, 2 * REACH:top - REACH]
+            out[REACH:frames - REACH, cols] = mid.astype(BF16)
+
+        for t, out in ((1, vg_ref), (0, kg_ref)):
             @pl.when(has_lo)
             def _():
                 rim(t, g, 0).wait_recv()
@@ -184,13 +190,48 @@
             def _():
                 rim_far(t, g, 1).wait_recv()
 
-            cols = pl.ds(pl.multiple_of(g * PAIR, PAIR), PAIR)
             own = totals[t, g, REACH:2 * REACH]
             out[:REACH, cols] = (own + in_rim[t, g, 0].astype(F32)).astype(BF16)
-            mid = totals[t, g, 2 * REACH:top - REACH]
-            out[REACH:frames - REACH, cols] = mid.astype(BF16)
             own = totals[t, g, top - REACH:top]
             out[frames - REACH:, cols] = (own + in_rim[t, g, 1].astype(F32)).astype(BF16)
+
+    def arrived(t, g):
+        @pl.when(has_lo)
+        def _():
+            halo(t, g, 0).wait_recv()
+
+        @pl.when(last)
+        def _():
+            halo_far(t, g, 0).wait_recv()
+
+        @pl.when(has_hi)
+        def _():
+            halo(t, g, 1).wait_recv()
+
+        @pl.when(first)
+        def _():
+            halo_far(t, g, 1).wait_recv()
+
+    def send_rims(t, g):
+        @pl.when(has_hi)
+        def _():
+            out_rim[t, g, 0, :NEAR] = totals[t, g, top:top + NEAR].astype(BF16)
+            rim(t, g, 0).start()
+
+        @pl.when(first)
+        def _():
+            out_rim[t, g, 0, NEAR:] = totals[t, g, top + NEAR:].astype(BF16)
+            rim_far(t, g, 0).start()
+
+        @pl.when(has_lo)
+        def _():
+            out_rim[t, g, 1, FAR:] = totals[t, g, FAR:REACH].astype(BF16)
+            rim(t, g, 1).start()
+
+        @pl.when(last)
+        def _():
+            out_rim[t, g, 1, :FAR] = totals[t, g, :FAR].astype(BF16)
+            rim_far(t, g, 1).start()
 
     def per_pair(g, _):
         cols = pl.ds(pl.multiple_of(g * PAIR, PAIR), PAIR)
@@ -209,22 +250,7 @@
             gt8[e] = jnp.where(mine_t, grad_t * 0.125, 0.0).astype(BF16)
             gm[e] = jnp.where(mine, grad, 0.0).astype(BF16)
 
-        for t in range(2):
-            @pl.when(has_lo)
-            def _():
-                halo(t, g, 0).wait_recv()
-
-            @pl.when(last)
-            def _():
-                halo_far(t, g, 0).wait_recv()
-
-            @pl.when(has_hi)
-            def _():
-                halo(t, g, 1).wait_recv()
-
-            @pl.when(first)
-            def _():
-                halo_far(t, g, 1).wait_recv()
+        arrived(0, g)
 
         def scores(i, carry):
             rows = rows_of(i)
@@ -264,7 +290,9 @@
             totals[1, g, rows] = term
             return 0
 
+        arrived(1, g)
         lax.fori_loop(0, chunks, attend, 0, unroll=UNROLL)
+        send_rims(1, g)
 
         attended = att_t[...].astype(BF16).astype(F32)
         att_ref[:, cols] = attended.T.astype(BF16)
@@ -289,28 +317,8 @@
             return 0
 
         lax.fori_loop(0, chunks, backward, 0, unroll=UNROLL)
+        send_rims(0, g)
         qg_ref[:, cols] = qg_t[...].T.astype(BF16)
-
-        for t in range(2):
-            @pl.when(has_hi)
-            def _():
-                out_rim[t, g, 0, :NEAR] = totals[t, g, top:top + NEAR].astype(BF16)
-                rim(t, g, 0).start()
-
-            @pl.when(first)
-            def _():
-                out_rim[t, g, 0, NEAR:] = totals[t, g, top + NEAR:].astype(BF16)
-                rim_far(t, g, 0).start()
-
-            @pl.when(has_lo)
-            def _():
-                out_rim[t, g, 1, FAR:] = totals[t, g, FAR:REACH].astype(BF16)
-                rim(t, g, 1).start()
-
-            @pl.when(last)
-            def _():
-                out_rim[t, g, 1, :FAR] = totals[t, g, :FAR].astype(BF16)
-                rim_far(t, g, 1).start()
 
         @pl.when(g > 0)
         def _():
@@ -348,6 +356,20 @@
             @pl.when(last)
             def _():
                 rim_far(t, g, 1).wait_send()
+
+
+def hand_on(*refs):
+    srcs, dsts, sem = refs[:4], refs[4:8], refs[8]
+    copies = []
+    for a in range(4):
+        part = srcs[a].shape[0] // PARTS
+        for b in range(PARTS):
+            rows = pl.ds(b * part, part)
+            copies.append(pltpu.make_async_copy(srcs[a].at[rows], dsts[a].at[rows], sem.at[a, b]))
+    for copy in copies:
+        copy.start()
+    for copy in copies:
+        copy.wait()
 
 
 def on_device(n, queries, keys, values, out_grad, band_start, band_len):
@@ -359,7 +381,7 @@
     vmem = pl.BlockSpec(memory_space=pltpu.VMEM)
     smem = pl.BlockSpec(memory_space=pltpu.SMEM)
     anywhere = pl.BlockSpec(memory_space=pl.ANY)
-    return pl.pallas_call(
+    results = pl.pallas_call(
         functools.partial(kernel, n),
         out_shape=(
             jax.ShapeDtypeStruct((units, width), BF16),
@@ -390,6 +412,14 @@
         ),
         name="banded",
     )(band_start, band_len, queries, out_grad, keys, values)
+    return pl.pallas_call(
+        hand_on,
+        out_shape=tuple(jax.ShapeDtypeStruct(r.shape, r.dtype) for r in results),
+        in_specs=[vmem] * 4,
+        out_specs=(anywhere,) * 4,
+        scratch_shapes=[dma((4, PARTS))],
+        name="hand_on",
+    )(*results)
 
 
 def solution(mesh):

time: 70.7 us -> 65.2 us (0.922)
  the two profiles are of different devices: /device:TPU:1 before, /device:TPU:14 now
where the time goes in v3:
time: 65.2 us; the launch traced here: 65 us
  Pallas kernels  64.4 us (99%)
    pallas_call x1, Pallas kernels, on_device(): pl.pallas_call(functools.partial(kernel, n), out_shape=(jax.ShapeDtypeStr...  60 us
    pallas_call x1, Pallas kernels, on_device(): pl.pallas_call(hand_on, out_shape=tuple((jax.ShapeDtypeStruct(r.shape, r....  4.34 us

profile of v3, /device:TPU:14, one launch (start us, length us, event | category | flops | bytes accessed | tf_op | source)
XLA Modules:
  0.0 65.0 jit_solution(13613690072052893078)
XLA Ops:
  0.6 60.0 %banded.1 = (bf16[512,512]{1,0:T(8,128)(2,1)}, bf16[512,512]{1,0:T(8,128)(2,1)}, bf16[1536,512]{1,0:T(8,128)(2,1)}, bf16[1536,512]{1,0:T(8,128)(2,1)}) custom-call(s32[16]{0:T(128)} %start_ref.1, s32[16]{0:T(128)} %len_ref.1, bf16[512,512]{1,0:T(8,128)(2,1)} %q_ref.1, bf16[512,512]{1,0:T(8,128)(2,1)} %g_ref.1, bf16[1536,512]{1,0:T(8,128)(2,1)} %k_hbm.1, ...), custom_call_target="tpu_custom_call" | custom-call | tf_op jit(solution)/shard_map/banded/pallas_call | solution.py:384
  60.7 4.3 %hand_on.1 = (bf16[512,512]{1,0:T(8,128)(2,1)}, bf16[512,512]{1,0:T(8,128)(2,1)}, bf16[1536,512]{1,0:T(8,128)(2,1)}, bf16[1536,512]{1,0:T(8,128)(2,1)}) custom-call(bf16[512,512]{1,0:T(8,128)(2,1)} %get-tuple-element.8.refs_0_, bf16[512,512]{1,0:T(8,128)(2,1)} %get-tuple-element.9.refs_1_, bf16[1536,512]{1,0:T(8,128)(2,1)} %get-tuple-element.10.refs_2_, ...), custom_call_target="tpu_custom_call" | custom-call | tf_op jit(solution)/shard_map/hand_on/pallas_call | solution.py:415

commit v4 on v3

--- a/solution.py
+++ b/solution.py
@@ -14,8 +14,8 @@
 REACH = 512
 NEAR = 384
 FAR = REACH - NEAR
-CHUNK = 1152
-UNROLL = 1
+CHUNK = 384
+UNROLL = 6
 PARTS = 4
 EXPONENT = 0.125 * math.log2(math.e)
 MASKED = -1e30

time: 65.2 us -> 65 us (level)
  the two profiles are of different devices: /device:TPU:14 before, /device:TPU:1 now
where the time goes in v4:
time: 65 us; the launch traced here: 64.8 us
  Pallas kernels  64.2 us (99%)
    pallas_call x1, Pallas kernels, on_device(): pl.pallas_call(functools.partial(kernel, n), out_shape=(jax.ShapeDtypeStr...  59.8 us
    pallas_call x1, Pallas kernels, on_device(): pl.pallas_call(hand_on, out_shape=tuple((jax.ShapeDtypeStruct(r.shape, r....  4.34 us

profile of v4, /device:TPU:1, one launch (start us, length us, event | category | flops | bytes accessed | tf_op | source)
XLA Modules:
  0.0 64.8 jit_solution(14545069546516745597)
XLA Ops:
  0.6 59.8 %banded.1 = (bf16[512,512]{1,0:T(8,128)(2,1)}, bf16[512,512]{1,0:T(8,128)(2,1)}, bf16[1536,512]{1,0:T(8,128)(2,1)}, bf16[1536,512]{1,0:T(8,128)(2,1)}) custom-call(s32[16]{0:T(128)} %start_ref.1, s32[16]{0:T(128)} %len_ref.1, bf16[512,512]{1,0:T(8,128)(2,1)} %q_ref.1, bf16[512,512]{1,0:T(8,128)(2,1)} %g_ref.1, bf16[1536,512]{1,0:T(8,128)(2,1)} %k_hbm.1, ...), custom_call_target="tpu_custom_call" | custom-call | tf_op jit(solution)/shard_map/banded/pallas_call | solution.py:384
  60.5 4.3 %hand_on.1 = (bf16[512,512]{1,0:T(8,128)(2,1)}, bf16[512,512]{1,0:T(8,128)(2,1)}, bf16[1536,512]{1,0:T(8,128)(2,1)}, bf16[1536,512]{1,0:T(8,128)(2,1)}) custom-call(bf16[512,512]{1,0:T(8,128)(2,1)} %get-tuple-element.8.refs_0_, bf16[512,512]{1,0:T(8,128)(2,1)} %get-tuple-element.9.refs_1_, bf16[1536,512]{1,0:T(8,128)(2,1)} %get-tuple-element.10.refs_2_, ...), custom_call_target="tpu_custom_call" | custom-call | tf_op jit(solution)/shard_map/hand_on/pallas_call | solution.py:415
